TPU v7x, 512 devices: a whole 4x4x16 slice. The times are simulated.
512 devices in a mesh: grp: 16 (over z), dev: 32 (over x, y, core).
Axes of the slice: x: 4, y: 4, z: 16, core: 2. Of those that a mesh axis runs over, the one named last changes fastest.
Arguments:
- elem_stiff: bfloat16 [576, 1048576], P(None, ('grp', 'dev')), as said below
- density: float32 [1048576], P(('grp', 'dev')), may hold values from 0.05 to 1
- owner: int32 [131072, 1], P(('grp', 'dev')), may hold values from 0 to 31; in each aligned block of 256 rows (0 to 255, 256 to 511, ...) at most 16 rows name the same one
- agg_slot: int32 [131072], P(('grp', 'dev')), may hold values from 0 to 63
- par_octant: int32 [131072], P(('grp', 'dev')), may hold values from 0 to 7
- agg_octant: int32 [32768], P(('grp', 'dev')), may hold values from 0 to 7
- coarse_map: int32 [32768], P(('grp', 'dev')), may hold values from 0 to 15
Outputs:
- level_two: float32 [576, 32768], P(None, ('grp', 'dev'))
- coarse: float32 [576, 512], P(None, 'dev')
Inputs may be any that keep to these rules, and one draw needn't show every extreme that they name: Among the parents of one device no owner is named more than 16 times, a bound that some block reaches. `elem_stiff`: every element matrix is symmetric.
All inputs are finite; a program needn't handle non-finite values.
Results may differ from a plain program's by a relative error of at most 0.0003.
Values sent between devices are 32-bit elements; how exact they have to be, the bound alone decides.
A program may use at most 128 MiB of HBM per device.

v0:
```python
import jax
import jax.numpy as jnp
import numpy as np
from jax import lax
from jax.sharding import PartitionSpec as P


def prolong_table():
    table = np.zeros((8, 24, 24), np.float32)
    for octant in range(8):
        for child in range(8):
            for corner in range(8):
                value = 1.0
                for bit in range(3):
                    place = ((octant >> bit & 1) + (child >> bit & 1)) / 2.0
                    value = value * (place if corner >> bit & 1 else 1.0 - place)
                for comp in range(3):
                    table[octant, child * 3 + comp, corner * 3 + comp] = value
    return jnp.asarray(table)


def lift_cols(stiff, octants, table):
    count = stiff.shape[1]
    picks = (octants[None, :] == jnp.arange(8, dtype=jnp.int32)[:, None]).astype(jnp.float32)
    select = jnp.einsum("oia,on->ian", table, picks, precision=lax.Precision.HIGHEST)
    mats = stiff.reshape(24, 24, count)
    left = jnp.einsum("ijn,jbn->ibn", mats, select, precision=lax.Precision.HIGHEST)
    return jnp.einsum("ian,ibn->abn", select, left, precision=lax.Precision.HIGHEST).reshape(
        576, count
    )


def coarse_terms(level_mats, octants, targets, table, width):
    lifted = lift_cols(level_mats, octants, table)
    into = (targets[:, None] == jnp.arange(width, dtype=jnp.int32)[None, :]).astype(jnp.float32)
    return jnp.dot(lifted, into, precision=lax.Precision.HIGHEST)


def body(elem_stiff, density, owner, agg_slot, par_octant, agg_octant, coarse_map):
    table = prolong_table()
    elem_dev = elem_stiff.shape[1]
    par_dev = elem_dev // 8
    agg_dev = agg_octant.shape[0]
    width = max(2, agg_dev // 4)
    weight = 0.001 + 0.999 * density * density * density
    mats = elem_stiff.reshape(24, 24, par_dev, 8)
    right = jnp.einsum(
        "ijqo,ojb->ibqo", mats, table.astype(jnp.bfloat16), preferred_element_type=jnp.float32
    )
    right = right * weight.reshape(par_dev, 8)[None, None]
    parent_mat = jnp.einsum("oia,ibqo->abq", table, right, precision=lax.Precision.HIGHEST)
    sent = lift_cols(parent_mat.reshape(576, par_dev), par_octant, table)
    peers = lax.axis_size("dev")
    slots = max(2, 2 * par_dev // peers)
    target = owner[:, 0]
    hits = (target[:, None] == jnp.arange(peers, dtype=jnp.int32)[None, :]).astype(jnp.int32)
    rank = jnp.sum(jnp.cumsum(hits, axis=0) * hits, axis=1) - 1
    place = target * slots + rank
    select = place[:, None] == jnp.arange(peers * slots, dtype=jnp.int32)[None, :]
    codes = (jnp.sum(jnp.where(select, agg_slot[:, None] + 1, 0), axis=0) - 1)[None, :]
    outgoing = jnp.dot(sent, select.astype(jnp.float32), precision=lax.Precision.HIGHEST)
    incoming, in_codes = (
        lax.all_to_all(outgoing, "dev", split_axis=1, concat_axis=1, tiled=True),
        lax.all_to_all(codes, "dev", split_axis=1, concat_axis=1, tiled=True),
    )
    into = (in_codes[0][:, None] == jnp.arange(agg_dev, dtype=jnp.int32)[None, :]).astype(
        jnp.float32
    )
    level_two = jnp.dot(incoming, into, precision=lax.Precision.HIGHEST)
    local = coarse_terms(level_two, agg_octant, coarse_map, table, width)
    coarse = lax.psum(local, "grp")
    return (level_two, coarse)


def solution(mesh):
    return jax.shard_map(
        body,
        mesh=mesh,
        in_specs=(
            P(None, ("grp", "dev")),
            P(("grp", "dev")),
            P(("grp", "dev"), None),
            P(("grp", "dev")),
            P(("grp", "dev")),
            P(("grp", "dev")),
            P(("grp", "dev")),
        ),
        out_specs=(P(None, ("grp", "dev")), P(None, "dev")),
        check_vma=False,
    )
```

profile of v0, /device:TPU:6, one launch (start us, length us, event | category | flops | bytes accessed | tf_op | source)
XLA Modules:
  0.0 167.0 jit_solution(16523208032190955235)
XLA Ops:
  0.6 0.7 fusion.20
  2.1 0.8 fusion.19
  2.9 0.7 multiply_add_fusion.1
  3.6 0.7 broadcast_add_fusion.1
  4.4 0.7 sub.15
  5.1 9.5 %all-to-all-start.1 = ((s32[1,32,16]{2,0,1:T(1,128)}), s32[1,32,16]{2,0,1:T(1,128)S(1)}, u32[]{:S(2)}, u32[]{:S(2)}) async-start(s32[1,32,16]{2,0,1:T(1,128)} %bitcast.17), calls=%async_computation.1 | async-start | bytes 32768 | tf_op jit(solution)/shard_map/all_to_all | solution.py:64
  14.6 2.2 %fusion.25 = f32[24,24,256]{2,1,0:T(8,128)} fusion(f32[8,24,24]{2,0,1:T(8,128)} %constant.22.clone, s32[256]{0:T(256)} %param.12), kind=kOutput, calls=%fused_computation.35 | convolution fusion | flops 14157824 | bytes 609280 | tf_op jit(solution)/shard_map/oia,on->ian/dot_general | solution.py:25
  16.8 2.1 %copy.45 = f32[24,24,256]{1,0,2:T(8,128)S(1)} copy(f32[24,24,256]{2,1,0:T(8,128)} %fusion.25) | data formatting | bytes 1179648 | tf_op jit(solution)/shard_map/oia,on->ian/dot_general | solution.py:25
  19.1 4.4 %copy.38 = bf16[576,2048]{0,1:T(8,128)(2,1)} copy(bf16[576,2048]{1,0:T(8,128)(2,1)} %param.8) | data formatting | bytes 4718592 | tf_op args[0]
  23.5 15.4 %reshape.84 = bf16[24,24,256,8]{1,0,3,2:T(8,128)(2,1)} reshape(bf16[576,2048]{0,1:T(8,128)(2,1)} %copy.38) | data formatting | bytes 4718592 | tf_op jit(solution)/shard_map/reshape | solution.py:46
  38.9 9.6 %bitcast_multiply_fusion = f32[24,24,256,8]{2,1,0,3:T(8,128)S(1)} fusion(f32[256,8]{0,1:T(8,128)S(1)} %copy.40, bf16[8,24,24,1]{1,2,3,0:T(8,128)(2,1)S(1)} %copy-done.3, bf16[24,24,256,8]{1,0,3,2:T(8,128)(2,1)} %reshape.84), kind=kOutput, calls=%fused_computation.2 | convolution fusion | flops 57802752 | bytes 7095296 | tf_op jit(solution)/shard_map/ijqo,ojb->ibqo/dot_general | solution.py:47
  48.5 5.4 %fusion.11 = f32[24,24,256]{2,0,1:T(8,128)} fusion(f32[8,24,24,1]{1,2,0,3:T(8,128)S(1)} %copy-done.2, f32[24,24,256,8]{2,1,0,3:T(8,128)S(1)} %bitcast_multiply_fusion), kind=kOutput, calls=%fused_computation.10 | convolution fusion | flops 339738624 | bytes 5326848 | tf_op jit(solution)/shard_map/oia,ibqo->abq/dot_general | solution.py:51
  54.0 3.1 %copy.44 = f32[24,24,256]{1,0,2:T(8,128)} copy(f32[24,24,256]{2,0,1:T(8,128)} %fusion.11) | data formatting | bytes 1179648 | tf_op jit(solution)/shard_map/oia,ibqo->abq/dot_general | solution.py:51
  57.1 7.4 %fusion.32 = f32[256,24,24]{2,1,0:T(8,128)S(1)} fusion(f32[24,24,256]{1,0,2:T(8,128)S(1)} %copy.45, f32[24,24,256]{1,0,2:T(8,128)} %copy.44), kind=kOutput, calls=%fused_computation.45 | convolution fusion | flops 42467328 | bytes 1769472 | tf_op jit(solution)/shard_map/ijn,jbn->ibn/dot_general | solution.py:27
  64.5 6.8 %fusion.8 = f32[24,24,256]{0,1,2:T(8,128)} fusion(f32[24,24,256]{1,0,2:T(8,128)S(1)} %copy.45, f32[256,24,24]{2,1,0:T(8,128)S(1)} %fusion.32), kind=kOutput, calls=%fused_computation.7 | convolution fusion | flops 42467328 | bytes 1769472 | tf_op jit(solution)/shard_map/ian,ibn->abn/dot_general | solution.py:28
  71.2 2.6 %copy.46 = f32[24,24,256]{2,1,0:T(8,128)S(1)} copy(f32[24,24,256]{0,1,2:T(8,128)} %fusion.8) | data formatting | bytes 1179648 | tf_op jit(solution)/shard_map/ian,ibn->abn/transpose | solution.py:28
  74.0 2.0 %fusion.14 = f32[576,32,16]{0,2,1:T(8,128)} fusion(f32[576,256,1]{1,0,2:T(8,128)S(1)} %bitcast.70, pred[32,16,256]{2,0,1:T(32,128)(4,1)S(1)} %broadcast_compare_fusion), kind=kOutput, calls=%fused_computation.13 | convolution fusion | flops 905969664 | bytes 1900544 | tf_op jit(solution)/shard_map/dot_general | solution.py:61
  76.0 7.4 %all-to-all-start = ((f32[576,32,16]{0,2,1:T(8,128)}), f32[576,32,16]{0,2,1:T(8,128)S(1)}, u32[]{:S(2)}, u32[]{:S(2)}) async-start(f32[576,32,16]{0,2,1:T(8,128)} %fusion.14), calls=%async_computation | async-start | bytes 2621440 | tf_op jit(solution)/shard_map/all_to_all | solution.py:63
  84.7 0.7 reduce.5
  85.4 16.0 %all-to-all-done = f32[576,32,16]{0,2,1:T(8,128)S(1)} async-done(((f32[576,32,16]{0,2,1:T(8,128)}), f32[576,32,16]{0,2,1:T(8,128)S(1)}, u32[]{:S(2)}, u32[]{:S(2)}) %all-to-all-start) | async-done | bytes 1179680 | tf_op jit(solution)/shard_map/all_to_all | solution.py:63
  101.4 0.7 fusion.16
  102.6 1.5 convolution_bitcast_fusion.1
  104.1 1.4 convolution_bitcast_fusion
  106.1 60.8 %psum.7 = f32[576,16]{0,1:T(8,128)} all-reduce(f32[576,16]{0,1:T(8,128)S(1)} %fusion.21), channel_id=1, replica_groups=mesh['grp'=16,'dev'=32] {'grp'}, use_global_device_ids=true, to_apply=%region_4.5 | all-reduce | flops 9216 | bytes 73728 | tf_op jit(solution)/shard_map/psum | solution.py:71
  (35 shorter events, 3.7 us)
Async XLA Ops:
  0.6 18.3 %copy-start.4 = (f32[2048]{0:T(1024)S(1)}, f32[2048]{0:T(1024)}, u32[]{:S(2)}) copy-start(f32[2048]{0:T(1024)} %param.9) | copy-start | bytes 24580
  5.1 70.8 %all-to-all-start.1 = ((s32[1,32,16]{2,0,1:T(1,128)}), s32[1,32,16]{2,0,1:T(1,128)S(1)}, u32[]{:S(2)}, u32[]{:S(2)}) async-start(s32[1,32,16]{2,0,1:T(1,128)} %bitcast.17), calls=%async_computation.1 | async-start | bytes 32768 | tf_op jit(solution)/shard_map/all_to_all | solution.py:64
  23.5 15.4 %copy-start.3 = (bf16[8,24,24,1]{1,2,3,0:T(8,128)(2,1)S(1)}, bf16[8,24,24,1]{1,2,3,0:T(8,128)(2,1)}, u32[]{:S(2)}) copy-start(bf16[8,24,24,1]{1,2,3,0:T(8,128)(2,1)} %constant.31) | copy-start | bytes 27652
  38.9 9.6 %copy-start.2 = (f32[8,24,24,1]{1,2,0,3:T(8,128)S(1)}, f32[8,24,24,1]{1,2,0,3:T(8,128)}, u32[]{:S(2)}) copy-start(f32[8,24,24,1]{1,2,0,3:T(8,128)} %constant.30) | copy-start | bytes 55300
  73.8 9.5 %copy-start.1 = (f32[8,24,24]{2,0,1:T(8,128)S(1)}, f32[8,24,24]{2,0,1:T(8,128)}, u32[]{:S(2)}) copy-start(f32[8,24,24]{2,0,1:T(8,128)} %constant.22.clone) | copy-start | bytes 55300
  73.8 9.5 %copy-start.5 = (s32[64]{0:T(128)S(1)}, s32[64]{0:T(128)}, u32[]{:S(2)}) copy-start(s32[64]{0:T(128)} %param.13) | copy-start | bytes 772
  76.0 25.5 %all-to-all-start = ((f32[576,32,16]{0,2,1:T(8,128)}), f32[576,32,16]{0,2,1:T(8,128)S(1)}, u32[]{:S(2)}, u32[]{:S(2)}) async-start(f32[576,32,16]{0,2,1:T(8,128)} %fusion.14), calls=%async_computation | async-start | bytes 2621440 | tf_op jit(solution)/shard_map/all_to_all | solution.py:63
  102.1 3.7 %copy-start = (f32[576,64]{0,1:T(8,128)}, f32[576,64]{0,1:T(8,128)S(1)}, u32[]{:S(2)}) copy-start(f32[576,64]{0,1:T(8,128)S(1)} %fusion.16) | copy-start | bytes 442372
  102.6 3.2 %copy-start.6 = (s32[64]{0:T(128)S(1)}, s32[64]{0:T(128)}, u32[]{:S(2)}) copy-start(s32[64]{0:T(128)} %param.14) | copy-start | bytes 772
where the time goes:
time: 168 us; the launch traced here: 167 us
  blocking collectives  60.8 us (36%)
  matrix products  37.7 us (22%)
  local copies, waits for them, and re-layouts  30.3 us (18%)
  starting transfers between devices  16.9 us (10%)
  waiting for transfers between devices  16 us (10%)
  other arithmetic  4.44 us (3%)
    psum x1, blocking collectives, body(): coarse = lax.psum(local, 'grp')  60.8 us
    all_to_all x1, waiting for transfers between devices, body(): lax.all_to_all(outgoing, 'dev', split_axis=1, concat_axis=1, tiled=True)  16 us
    reshape x1, local copies, waits for them, and re-layouts, body(): mats = elem_stiff.reshape(24, 24, par_dev, 8)  15.4 us
    dot_general x1, matrix products, body(): jnp.einsum('ijqo,ojb->ibqo', mats, table.astype(jnp.bfloat16), preferred_...  9.64 us
    all_to_all x1, starting transfers between devices, body(): lax.all_to_all(codes, 'dev', split_axis=1, concat_axis=1, tiled=True)  9.49 us
    dot_general x2, matrix products, lift_cols(): jnp.einsum('ijn,jbn->ibn', mats, select, precision=lax.Precision.HIGHEST)  8.91 us
    dot_general x2, matrix products, lift_cols(): jnp.einsum('ian,ibn->abn', select, left, precision=lax.Precision.HIGHEST)  8.15 us
    all_to_all x1, starting transfers between devices, body(): lax.all_to_all(outgoing, 'dev', split_axis=1, concat_axis=1, tiled=True)  7.38 us
  transfers between devices with their start and end apart: 2, of which 1 were waited for; matrix products, arithmetic and copies ran while one was open for 38% of the time, Pallas kernels for 0%

commit v1 on v0

v1 whole, which is shorter than its diff:
```python
import functools

import jax
import jax.numpy as jnp
import ml_dtypes
import numpy as np
from jax import lax
from jax.experimental import pallas as pl
from jax.experimental.pallas import tpu as pltpu
from jax.sharding import PartitionSpec as P

MESH = pl.DeviceIdType.MESH
F32, BF16 = jnp.float32, jnp.bfloat16
MODES = 300
CODE = 300
COLS = 304
WIDE = 384
KEEP = ((0, 384), (400, 432), (448, 480), (496, 528), (544, 576))
SLOTS = 16
PACK = 40


def prolong_np():
    table = np.zeros((8, 24, 24))
    for octant in range(8):
        for child in range(8):
            for corner in range(8):
                value = 1.0
                for bit in range(3):
                    place = (((octant >> bit) & 1) + ((child >> bit) & 1)) / 2.0
                    value *= place if (corner >> bit) & 1 else 1.0 - place
                for comp in range(3):
                    table[octant, child * 3 + comp, corner * 3 + comp] = value
    return table


def constants():
    table = prolong_np()
    axis = np.array([[1.0, -1.0], [1.0, 1.0]])
    basis = np.kron(np.kron(np.kron(axis, axis), axis), np.eye(3))
    pairs = [(k, l) for k in range(24) for l in range(k, 24)]
    ks, ls = np.array([p[0] for p in pairs]), np.array([p[1] for p in pairs])
    kept = np.concatenate([np.arange(a, b) for a, b in KEEP])
    row_i, row_j = kept // 24, kept % 24
    used = row_i <= row_j
    off = (row_i != row_j)[None, :]
    first = np.zeros((8, COLS, kept.size))
    for octant in range(8):
        modes = table[octant] @ basis
        term = modes[row_i][:, ks].T * modes[row_j][:, ls].T
        swap = modes[row_j][:, ks].T * modes[row_i][:, ls].T
        first[octant, :MODES] = np.where(used[None, :], term + off * swap, 0.0)
    step = np.linalg.inv(basis) @ table[7] @ basis
    lift = np.zeros((WIDE, WIDE))
    lift[:MODES, :MODES] = step[ks][:, ks].T * step[ls][:, ls].T + (ks != ls)[None, :] * (step[ls][:, ks].T * step[ks][:, ls].T)
    signs = np.zeros((WIDE, 8))
    parity = (ks // 3) ^ (ls // 3)
    for octant in range(8):
        sign = np.ones(MODES)
        for bit in range(3):
            sign *= np.where((parity >> bit) & 1, 1.0 if (octant >> bit) & 1 else -1.0, 1.0)
        signs[:MODES, octant] = sign
    nodal = np.zeros((576, WIDE))
    a, b = np.arange(576) // 24, np.arange(576) % 24
    nodal[:, :MODES] = (basis[a][:, ks] * basis[b][:, ls] + (ks != ls)[None, :] * basis[a][:, ls] * basis[b][:, ks]) / 64.0
    cast = lambda array: np.asarray(array).astype(ml_dtypes.bfloat16)
    return cast(first), cast(lift), cast(signs), cast(nodal)


def mm(left, right, left_dim=1, right_dim=0):
    return lax.dot_general(left, right, (((left_dim,), (right_dim,)), ((), ())), preferred_element_type=F32)


def iota(shape, dim):
    return lax.broadcasted_iota(jnp.int32, shape, dim)


def halves(value):
    high = value.astype(BF16)
    return high, (value - high.astype(F32)).astype(BF16)


def ones_where(mask):
    return jnp.where(mask, 1.0, 0.0).astype(BF16)


def kernel(
    n_grp, n_dev,
    stiff, dens, owner, slot, par_oct, agg_oct, agg_map, first, lift, signs, nodal,
    level_out, coarse_out,
    stiff_v, dens_v, owner_v, slot_v, par_oct_v, agg_oct_v, agg_map_v, first_v, lift_v, signs_v, nodal_v,
    xt, outgo, income, parts, gathered, totals,
    in_sem, first_sem, stiff_sem, send_sem, recv_sem, part_send, part_recv, total_send, total_recv,
):
    me_g, me_d = lax.axis_index("grp"), lax.axis_index("dev")
    blocks = 8

    loads = []
    for index, (src, dst) in enumerate((
        (dens, dens_v), (owner, owner_v), (slot, slot_v), (par_oct, par_oct_v), (agg_oct, agg_oct_v),
        (agg_map, agg_map_v), (lift, lift_v), (signs, signs_v), (nodal, nodal_v),
    )):
        loads.append(pltpu.make_async_copy(src, dst, in_sem.at[index]))
    stiff_loads = [
        pltpu.make_async_copy(stiff.at[:, pl.ds(512 * c, 512)], stiff_v.at[:, pl.ds(512 * c, 512)], stiff_sem.at[c])
        for c in range(4)
    ]
    first_loads = [pltpu.make_async_copy(first.at[o], first_v.at[o], first_sem.at[o]) for o in range(8)]
    for load in loads[:6] + stiff_loads + loads[6:8] + first_loads + loads[8:]:
        load.start()

    barrier = pltpu.get_barrier_semaphore()

    def greet_dev(k, _):
        pl.semaphore_signal(barrier, inc=1, device_id={"dev": lax.rem(me_d + k, n_dev)}, device_id_type=MESH)
        return 0

    def greet_grp(k, _):
        pl.semaphore_signal(barrier, inc=1, device_id={"grp": lax.rem(me_g + k, n_grp)}, device_id_type=MESH)
        return 0

    lax.fori_loop(1, n_dev, greet_dev, 0)
    lax.fori_loop(1, n_grp, greet_grp, 0)

    for load in loads[:6]:
        load.wait()

    owner_row = owner_v[...]
    hits = iota((n_dev, 256), 0) == owner_row
    before = ones_where(iota((256, 256), 0) < iota((256, 256), 1))
    hits_f = jnp.where(hits, 1.0, 0.0)
    rank = jnp.sum(mm(hits_f.astype(BF16), before) * hits_f, axis=0, keepdims=True)
    place = owner_row * SLOTS + rank.astype(jnp.int32)
    code = slot_v[...].astype(F32) + 1.0

    pos = iota((256, 256), 0)
    perm = ones_where(iota((256, 256), 1) == 8 * (pos % 32) + pos // 32)

    dens_row = dens_v[...]
    dens_8 = jnp.concatenate([dens_row[:, 256 * b:256 * (b + 1)] for b in range(blocks)], axis=0)
    weight = 0.001 + 0.999 * dens_8 * dens_8 * dens_8
    one = weight.astype(BF16)
    rest = weight - one.astype(F32)
    two = rest.astype(BF16)
    three = (rest - two.astype(F32)).astype(BF16)
    pieces = jnp.concatenate([one.astype(F32), two.astype(F32), three.astype(F32)], axis=0).astype(BF16)
    turned = mm(perm, pieces, 1, 1).astype(BF16)
    spread = ones_where(iota((24, 256), 0) % 8 == iota((24, 256), 1) // 32)
    spread_w = mm(turned, spread)
    own_row = iota((256, 256), 0) % 32 == iota((256, 256), 1) % 32
    weights = jnp.sum(jnp.where(own_row, spread_w, 0.0).reshape(8, 32, 256), axis=1)

    for c in range(4):
        stiff_loads[c].wait()
        for b in (2 * c, 2 * c + 1):
            lanes = slice(256 * b, 256 * (b + 1))
            block = jnp.concatenate([stiff_v[a:z, lanes] for a, z in KEEP], axis=0)
            rows = mm(perm, block, 1, 1).astype(BF16)
            for o in range(8):
                xt[o, 32 * b:32 * (b + 1), :] = rows[32 * o:32 * (o + 1)]

    parent = None
    for o in range(8):
        first_loads[o].wait()
        term = mm(first_v[o], xt[o], 1, 1) * weights[o:o + 1, :]
        parent = term if parent is None else parent + term

    for load in loads[6:8]:
        load.wait()
    octs = ones_where(iota((8, 256), 0) == par_oct_v[...])
    flips = mm(signs_v[0:COLS, :], octs)
    high, low = halves(parent * flips)
    lift_c = lift_v[0:COLS, 0:COLS]
    sent = (mm(lift_c, high) + mm(lift_c, low)) * flips
    sent = jnp.where(iota((COLS, 256), 0) == CODE, code, sent)
    tail = sent[256:COLS]
    gap = jnp.zeros((16, 256), F32)
    full = jnp.concatenate([sent, gap, tail, gap], axis=0)
    high, low = halves(full)

    picks = ones_where(iota((n_dev * SLOTS, 256), 0) == place)
    chosen = mm(picks, high, 1, 1) + mm(picks, low, 1, 1)
    outgo[:, 0:16, :] = chosen[:, 0:128].reshape(n_dev, 16, 128)
    outgo[:, 16:32, :] = chosen[:, 128:256].reshape(n_dev, 16, 128)
    ends = chosen[:, 256:384].reshape(n_dev, 2, 8, 128)
    outgo[:, 32:40, :] = jnp.where(iota((n_dev, 8, 128), 2) < 64, ends[:, 0], ends[:, 1])

    pl.semaphore_wait(barrier, n_dev + n_grp - 2)

    def to_owner(k):
        peer = lax.rem(me_d + k, n_dev)
        return pltpu.make_async_remote_copy(
            src_ref=outgo.at[peer], dst_ref=income.at[me_d], send_sem=send_sem.at[peer],
            recv_sem=recv_sem.at[me_d], device_id={"dev": peer}, device_id_type=MESH,
        )

    def from_source(k):
        peer = lax.rem(me_d + k, n_dev)
        return pltpu.make_async_remote_copy(
            src_ref=outgo.at[peer], dst_ref=income.at[peer], send_sem=send_sem.at[peer],
            recv_sem=recv_sem.at[peer], device_id={"dev": peer}, device_id_type=MESH,
        )

    def start_owner(k, _):
        to_owner(k).start()
        return 0

    def end_source(k, _):
        from_source(k).wait_recv()
        return 0

    def end_owner(k, _):
        to_owner(k).wait_send()
        return 0

    lax.fori_loop(1, n_dev, start_owner, 0)
    income[me_d] = outgo[me_d]

    octs = ones_where(iota((8, 64), 0) == agg_oct_v[...])
    agg_flips = mm(octs, signs_v[...], 0, 1)
    sums = ones_where(iota((16, 64), 0) == agg_map_v[...])
    loads[8].wait()

    lax.fori_loop(1, n_dev, end_source, 0)

    lane = iota((8, 128), 1)
    code_at = ones_where(lane == CODE - 256 + 64 * iota((8, 128), 0))
    packed = income[:, 32:40, :].reshape(n_dev * 8, 128)
    codes = mm(code_at, packed.astype(BF16), 1, 1).astype(jnp.int32)
    level = []
    for h in range(2):
        into = ones_where(iota((64, n_dev * 8), 0) == codes[h:h + 1, :] - 1)
        wide = jnp.concatenate([
            income[:, 8 * h:8 * h + 8, :].reshape(n_dev * 8, 128),
            income[:, 16 + 8 * h:24 + 8 * h, :].reshape(n_dev * 8, 128),
            packed,
        ], axis=1)
        high, low = halves(wide)
        level.append(mm(into, high) + mm(into, low))
    ends = level[0][:, 256:] + pltpu.roll(level[1][:, 256:], 64, 1)
    ends = jnp.where(iota((64, 128), 1) < MODES - 256, ends, 0.0)
    level = jnp.concatenate([level[0][:, :256] + level[1][:, :256], ends], axis=1)

    both = jnp.concatenate(halves(level * agg_flips), axis=0)
    lifted = mm(both, lift_v[...], 1, 1)
    high, low = halves((lifted[0:64] + lifted[64:128]) * agg_flips)
    share = mm(sums, high) + mm(sums, low)
    for k in range(3):
        parts[:, k, :] = share[:, 128 * k:128 * (k + 1)]

    def to_adder(k):
        peer = lax.rem(me_g + k, n_grp)
        return pltpu.make_async_remote_copy(
            src_ref=parts.at[peer], dst_ref=gathered.at[me_g], send_sem=part_send.at[peer],
            recv_sem=part_recv.at[me_g], device_id={"grp": peer}, device_id_type=MESH,
        )

    def from_slab(k):
        peer = lax.rem(me_g + k, n_grp)
        return pltpu.make_async_remote_copy(
            src_ref=parts.at[peer], dst_ref=gathered.at[peer], send_sem=part_send.at[peer],
            recv_sem=part_recv.at[peer], device_id={"grp": peer}, device_id_type=MESH,
        )

    def to_all(k):
        peer = lax.rem(me_g + k, n_grp)
        return pltpu.make_async_remote_copy(
            src_ref=totals.at[me_g], dst_ref=totals.at[me_g], send_sem=total_send.at[peer],
            recv_sem=total_recv.at[me_g], device_id={"grp": peer}, device_id_type=MESH,
        )

    def from_adder(k):
        peer = lax.rem(me_g + k, n_grp)
        return pltpu.make_async_remote_copy(
            src_ref=totals.at[me_g], dst_ref=totals.at[peer], send_sem=total_send.at[peer],
            recv_sem=total_recv.at[peer], device_id={"grp": peer}, device_id_type=MESH,
        )

    def loop(make, act):
        def run(k, _):
            getattr(make(k), act)()
            return 0
        lax.fori_loop(1, n_grp, run, 0)

    loop(to_adder, "start")
    gathered[me_g] = parts[me_g]

    high, low = halves(level)
    level_out[...] = mm(high, nodal_v[...], 1, 1) + mm(low, nodal_v[...], 1, 1)

    loop(from_slab, "wait_recv")
    totals[me_g] = jnp.sum(gathered[...], axis=0)
    loop(to_all, "start")
    lax.fori_loop(1, n_dev, end_owner, 0)
    loop(to_adder, "wait_send")
    loop(from_adder, "wait_recv")

    coarse = jnp.concatenate([totals[:, k, :] for k in range(3)], axis=1)
    high, low = halves(coarse)
    coarse_out[...] = mm(high, nodal_v[...], 1, 1) + mm(low, nodal_v[...], 1, 1)
    loop(to_all, "wait_send")


def body(n_grp, n_dev, elem_stiff, density, owner, agg_slot, par_octant, agg_octant, coarse_map):
    first, lift, signs, nodal = constants()
    row = lambda array: array.reshape(1, -1)
    args = (
        elem_stiff, row(density), row(owner), row(agg_slot), row(par_octant), row(agg_octant), row(coarse_map),
        jnp.asarray(first), jnp.asarray(lift), jnp.asarray(signs), jnp.asarray(nodal),
    )
    dma = pltpu.SemaphoreType.DMA
    level, coarse = pl.pallas_call(
        functools.partial(kernel, n_grp, n_dev),
        out_shape=(jax.ShapeDtypeStruct((64, 576), F32), jax.ShapeDtypeStruct((16, 576), F32)),
        in_specs=[pl.BlockSpec(memory_space=pl.ANY)] * len(args),
        out_specs=(pl.BlockSpec(memory_space=pltpu.VMEM), pl.BlockSpec(memory_space=pltpu.VMEM)),
        scratch_shapes=[pltpu.VMEM(a.shape, a.dtype) for a in args] + [
            pltpu.VMEM((8, 256, 512), BF16),
            pltpu.VMEM((n_dev, PACK, 128), F32),
            pltpu.VMEM((n_dev, PACK, 128), F32),
            pltpu.VMEM((n_grp, 3, 128), F32),
            pltpu.VMEM((n_grp, 3, 128), F32),
            pltpu.VMEM((n_grp, 3, 128), F32),
            dma((9,)), dma((8,)), dma((4,)), dma((n_dev,)), dma((n_dev,)),
            dma((n_grp,)), dma((n_grp,)), dma((n_grp,)), dma((n_grp,)),
        ],
        compiler_params=pltpu.CompilerParams(
            collective_id=0, has_side_effects=True, vmem_limit_bytes=48 * 1024 * 1024
        ),
    )(*args)
    return level.T, coarse.T


def solution(mesh):
    split = P(("grp", "dev"))
    return jax.shard_map(
        functools.partial(body, mesh.shape["grp"], mesh.shape["dev"]),
        mesh=mesh,
        in_specs=(P(None, ("grp", "dev")), split, P(("grp", "dev"), None), split, split, split, split),
        out_specs=(P(None, ("grp", "dev")), P(None, "dev")),
        check_vma=False,
    )
```

time: 168 us -> 57.8 us (0.34)
  the two profiles are of different devices: /device:TPU:6 before, /device:TPU:1 now
where the time goes in v1:
time: 57.8 us; the launch traced here: 57.4 us
  Pallas kernels  45.2 us (78%)
  local copies, waits for them, and re-layouts  11.6 us (20%)
  between operations  0.66 us (1%)
    pallas_call x1, Pallas kernels, body(): pl.pallas_call(functools.partial(kernel, n_grp, n_dev), out_shape=(jax.Sh...  45.2 us
    unnamed x24, local copies, waits for them, and re-layouts  11.6 us

profile of v1, /device:TPU:1, one launch (start us, length us, event | category | flops | bytes accessed | tf_op | source)
XLA Modules:
  0.0 57.4 jit_solution(16288389375585624778)
XLA Ops:
  0.6 0.0 copy-start
  0.6 1.7 %copy-done = bf16[8,304,512]{2,1,0:T(8,128)(2,1)S(1)} copy-done((bf16[8,304,512]{2,1,0:T(8,128)(2,1)S(1)}, bf16[8,304,512]{2,1,0:T(8,128)(2,1)}, u32[]{:S(2)}) %copy-start) | copy-done | bytes 2490392
  2.3 0.0 copy-start.1
  2.3 1.7 %copy-done.1 = bf16[576,2048]{1,0:T(8,128)(2,1)S(1)} copy-done((bf16[576,2048]{1,0:T(8,128)(2,1)S(1)}, bf16[576,2048]{1,0:T(8,128)(2,1)}, u32[]{:S(2)}) %copy-start.1) | copy-done | bytes 2359320
  4.0 0.0 copy-start.2
  4.0 1.0 %copy-done.2 = bf16[576,384]{1,0:T(8,128)(2,1)S(1)} copy-done((bf16[576,384]{1,0:T(8,128)(2,1)S(1)}, bf16[576,384]{1,0:T(8,128)(2,1)}, u32[]{:S(2)}) %copy-start.2) | copy-done | bytes 442392
  5.0 0.0 copy-start.3
  5.0 1.0 %copy-done.3 = bf16[384,384]{1,0:T(8,128)(2,1)S(1)} copy-done((bf16[384,384]{1,0:T(8,128)(2,1)S(1)}, bf16[384,384]{1,0:T(8,128)(2,1)}, u32[]{:S(2)}) %copy-start.3) | copy-done | bytes 294936
  6.0 0.0 copy-start.4
  6.0 0.9 %copy-done.4 = bf16[384,8]{1,0:T(8,128)(2,1)S(1)} copy-done((bf16[384,8]{1,0:T(8,128)(2,1)S(1)}, bf16[384,8]{1,0:T(8,128)(2,1)}, u32[]{:S(2)}) %copy-start.4) | copy-done | bytes 6168
  6.9 0.0 copy-start.5
  6.9 0.7 %copy-done.5 = f32[2048]{0:T(1024)S(1)} copy-done((f32[2048]{0:T(1024)S(1)}, f32[2048]{0:T(1024)}, u32[]{:S(2)}) %copy-start.5) | copy-done | bytes 8216
  7.6 0.0 copy-start.6
  7.6 0.7 %copy-done.6 = s32[256,1]{0,1:T(1,128)S(1)} copy-done((s32[256,1]{0,1:T(1,128)S(1)}, s32[256,1]{0,1:T(1,128)}, u32[]{:S(2)}) %copy-start.6) | copy-done | bytes 1048
  8.2 0.0 copy-start.7
  8.3 0.7 %copy-done.7 = s32[256]{0:T(256)S(1)} copy-done((s32[256]{0:T(256)S(1)}, s32[256]{0:T(256)}, u32[]{:S(2)}) %copy-start.7) | copy-done | bytes 1048
  8.9 0.0 copy-start.8
  8.9 0.7 %copy-done.8 = s32[256]{0:T(256)S(1)} copy-done((s32[256]{0:T(256)S(1)}, s32[256]{0:T(256)}, u32[]{:S(2)}) %copy-start.8) | copy-done | bytes 1048
  9.6 0.0 copy-start.9
  9.6 0.7 %copy-done.9 = s32[64]{0:T(128)S(1)} copy-done((s32[64]{0:T(128)S(1)}, s32[64]{0:T(128)}, u32[]{:S(2)}) %copy-start.9) | copy-done | bytes 280
  10.3 0.7 %copy-done.10 = s32[64]{0:T(128)S(1)} copy-done((s32[64]{0:T(128)S(1)}, s32[64]{0:T(128)}, u32[]{:S(2)}) %copy-start.10) | copy-done | bytes 280
  10.9 45.2 %shard_map.122 = (f32[64,576]{1,0:T(8,128)S(1)}, f32[16,576]{1,0:T(8,128)S(1)}) custom-call(bf16[576,2048]{1,0:T(8,128)(2,1)S(1)} %copy-done.1, f32[1,2048]{1,0:T(1,128)S(1)} %bitcast.10, s32[1,256]{1,0:T(1,128)S(1)} %bitcast.11, s32[1,256]{1,0:T(1,128)S(1)} %bitcast.12, s32[1,256]{1,0:T(1,128)S(1)} %bitcast.13, s32[1,64]{1,0:T(1,128)S(1)} %bitcast.14, ...), custom_call_target="tpu_custom_call" | custom-call | tf_op jit(solution)/shard_map/pallas_call | solution.py:312
  56.1 0.7 %copy.15 = f32[576,64]{0,1:T(8,128)} copy(f32[576,64]{0,1:T(8,128)S(1)} %bitcast.8) | data formatting | bytes 294912
  56.8 0.6 %copy.16 = f32[576,16]{0,1:T(8,128)} copy(f32[576,16]{0,1:T(8,128)S(1)} %bitcast.9) | data formatting | bytes 73728
  (1 shorter events, 0.0 us)
Async XLA Ops:
  0.6 1.7 %copy-start = (bf16[8,304,512]{2,1,0:T(8,128)(2,1)S(1)}, bf16[8,304,512]{2,1,0:T(8,128)(2,1)}, u32[]{:S(2)}) copy-start(bf16[8,304,512]{2,1,0:T(8,128)(2,1)} %constant.8.clone.first) | copy-start | bytes 7471108
  2.3 1.7 %copy-start.1 = (bf16[576,2048]{1,0:T(8,128)(2,1)S(1)}, bf16[576,2048]{1,0:T(8,128)(2,1)}, u32[]{:S(2)}) copy-start(bf16[576,2048]{1,0:T(8,128)(2,1)} %stiff.1) | copy-start | bytes 7077892
  4.0 1.0 %copy-start.2 = (bf16[576,384]{1,0:T(8,128)(2,1)S(1)}, bf16[576,384]{1,0:T(8,128)(2,1)}, u32[]{:S(2)}) copy-start(bf16[576,384]{1,0:T(8,128)(2,1)} %constant.11.clone.nodal) | copy-start | bytes 1327108
  5.0 1.0 %copy-start.3 = (bf16[384,384]{1,0:T(8,128)(2,1)S(1)}, bf16[384,384]{1,0:T(8,128)(2,1)}, u32[]{:S(2)}) copy-start(bf16[384,384]{1,0:T(8,128)(2,1)} %constant.9.clone.lift) | copy-start | bytes 884740
  6.0 0.9 %copy-start.4 = (bf16[384,8]{1,0:T(8,128)(2,1)S(1)}, bf16[384,8]{1,0:T(8,128)(2,1)}, u32[]{:S(2)}) copy-start(bf16[384,8]{1,0:T(8,128)(2,1)} %constant.10.clone.signs) | copy-start | bytes 18436
  6.9 0.7 %copy-start.5 = (f32[2048]{0:T(1024)S(1)}, f32[2048]{0:T(1024)}, u32[]{:S(2)}) copy-start(f32[2048]{0:T(1024)} %param.12) | copy-start | bytes 24580
  7.6 0.7 %copy-start.6 = (s32[256,1]{0,1:T(1,128)S(1)}, s32[256,1]{0,1:T(1,128)}, u32[]{:S(2)}) copy-start(s32[256,1]{0,1:T(1,128)} %param.13) | copy-start | bytes 3076
  8.2 0.7 %copy-start.7 = (s32[256]{0:T(256)S(1)}, s32[256]{0:T(256)}, u32[]{:S(2)}) copy-start(s32[256]{0:T(256)} %param.14) | copy-start | bytes 3076
  8.9 0.7 %copy-start.8 = (s32[256]{0:T(256)S(1)}, s32[256]{0:T(256)}, u32[]{:S(2)}) copy-start(s32[256]{0:T(256)} %param.15) | copy-start | bytes 3076
  9.6 0.7 %copy-start.9 = (s32[64]{0:T(128)S(1)}, s32[64]{0:T(128)}, u32[]{:S(2)}) copy-start(s32[64]{0:T(128)} %param.16) | copy-start | bytes 772
  10.3 0.7 %copy-start.10 = (s32[64]{0:T(128)S(1)}, s32[64]{0:T(128)}, u32[]{:S(2)}) copy-start(s32[64]{0:T(128)} %param.17) | copy-start | bytes 772

commit v2 on v1

--- a/solution.py
+++ b/solution.py
@@ -17,6 +17,11 @@
 WIDE = 384
 KEEP = ((0, 384), (400, 432), (448, 480), (496, 528), (544, 576))
 SLOTS = 16
+FAR_FIRST = sorted(
+    [(dx, dy, dc) for dx in range(4) for dy in range(4) for dc in range(2) if dx + dy + dc],
+    key=lambda step: -(min(step[0], 4 - step[0]) + min(step[1], 4 - step[1])),
+)
+TEAM = 4
 PACK = 40
 
 
@@ -102,10 +107,10 @@
     )):
         loads.append(pltpu.make_async_copy(src, dst, in_sem.at[index]))
     stiff_loads = [
-        pltpu.make_async_copy(stiff.at[:, pl.ds(512 * c, 512)], stiff_v.at[:, pl.ds(512 * c, 512)], stiff_sem.at[c])
-        for c in range(4)
+        pltpu.make_async_copy(stiff.at[:, pl.ds(1024 * c, 1024)], stiff_v.at[:, pl.ds(1024 * c, 1024)], stiff_sem.at[c])
+        for c in range(2)
     ]
-    first_loads = [pltpu.make_async_copy(first.at[o], first_v.at[o], first_sem.at[o]) for o in range(8)]
+    first_loads = [pltpu.make_async_copy(first, first_v, first_sem.at[0])]
     for load in loads[:6] + stiff_loads + loads[6:8] + first_loads + loads[8:]:
         load.start()
 
@@ -150,9 +155,9 @@
     own_row = iota((256, 256), 0) % 32 == iota((256, 256), 1) % 32
     weights = jnp.sum(jnp.where(own_row, spread_w, 0.0).reshape(8, 32, 256), axis=1)
 
-    for c in range(4):
+    for c in range(2):
         stiff_loads[c].wait()
-        for b in (2 * c, 2 * c + 1):
+        for b in range(4 * c, 4 * c + 4):
             lanes = slice(256 * b, 256 * (b + 1))
             block = jnp.concatenate([stiff_v[a:z, lanes] for a, z in KEEP], axis=0)
             rows = mm(perm, block, 1, 1).astype(BF16)
@@ -160,13 +165,13 @@
                 xt[o, 32 * b:32 * (b + 1), :] = rows[32 * o:32 * (o + 1)]
 
     parent = None
+    first_loads[0].wait()
+    for load in loads[6:8]:
+        load.wait()
     for o in range(8):
-        first_loads[o].wait()
         term = mm(first_v[o], xt[o], 1, 1) * weights[o:o + 1, :]
         parent = term if parent is None else parent + term
 
-    for load in loads[6:8]:
-        load.wait()
     octs = ones_where(iota((8, 256), 0) == par_oct_v[...])
     flips = mm(signs_v[0:COLS, :], octs)
     high, low = halves(parent * flips)
@@ -187,33 +192,29 @@
 
     pl.semaphore_wait(barrier, n_dev + n_grp - 2)
 
-    def to_owner(k):
-        peer = lax.rem(me_d + k, n_dev)
+    def to_owner(peer):
         return pltpu.make_async_remote_copy(
             src_ref=outgo.at[peer], dst_ref=income.at[me_d], send_sem=send_sem.at[peer],
             recv_sem=recv_sem.at[me_d], device_id={"dev": peer}, device_id_type=MESH,
         )
 
-    def from_source(k):
-        peer = lax.rem(me_d + k, n_dev)
+    def from_source(peer):
         return pltpu.make_async_remote_copy(
             src_ref=outgo.at[peer], dst_ref=income.at[peer], send_sem=send_sem.at[peer],
             recv_sem=recv_sem.at[peer], device_id={"dev": peer}, device_id_type=MESH,
         )
 
-    def start_owner(k, _):
-        to_owner(k).start()
-        return 0
-
     def end_source(k, _):
-        from_source(k).wait_recv()
+        from_source(lax.rem(me_d + k, n_dev)).wait_recv()
         return 0
 
     def end_owner(k, _):
-        to_owner(k).wait_send()
-        return 0
-
-    lax.fori_loop(1, n_dev, start_owner, 0)
+        to_owner(lax.rem(me_d + k, n_dev)).wait_send()
+        return 0
+
+    x, y, core = lax.div(me_d, 8), lax.rem(lax.div(me_d, 2), 4), lax.rem(me_d, 2)
+    for dx, dy, dc in FAR_FIRST:
+        to_owner((lax.rem(x + dx, 4) * 4 + lax.rem(y + dy, 4)) * 2 + lax.rem(core + dc, 2)).start()
     income[me_d] = outgo[me_d]
 
     octs = ones_where(iota((8, 64), 0) == agg_oct_v[...])
@@ -245,60 +246,61 @@
     lifted = mm(both, lift_v[...], 1, 1)
     high, low = halves((lifted[0:64] + lifted[64:128]) * agg_flips)
     share = mm(sums, high) + mm(sums, low)
-    for k in range(3):
-        parts[:, k, :] = share[:, 128 * k:128 * (k + 1)]
-
-    def to_adder(k):
+    for t in range(TEAM):
+        for k in range(3):
+            parts[t, 4 * k:4 * k + 4, :] = share[4 * t:4 * t + 4, 128 * k:128 * (k + 1)]
+
+    mine = lax.rem(me_g, TEAM)
+    base = me_g - mine
+
+    def in_team(k, sending):
+        other = lax.rem(mine + k, TEAM)
+        return pltpu.make_async_remote_copy(
+            src_ref=parts.at[other], dst_ref=gathered.at[mine if sending else other], send_sem=part_send.at[other],
+            recv_sem=part_recv.at[mine if sending else other], device_id={"grp": base + other}, device_id_type=MESH,
+        )
+
+    def to_all(k, sending):
         peer = lax.rem(me_g + k, n_grp)
         return pltpu.make_async_remote_copy(
-            src_ref=parts.at[peer], dst_ref=gathered.at[me_g], send_sem=part_send.at[peer],
-            recv_sem=part_recv.at[me_g], device_id={"grp": peer}, device_id_type=MESH,
+            src_ref=totals.at[me_g], dst_ref=totals.at[me_g if sending else peer], send_sem=total_send.at[peer],
+            recv_sem=total_recv.at[me_g if sending else peer], device_id={"grp": peer}, device_id_type=MESH,
         )
 
-    def from_slab(k):
-        peer = lax.rem(me_g + k, n_grp)
-        return pltpu.make_async_remote_copy(
-            src_ref=parts.at[peer], dst_ref=gathered.at[peer], send_sem=part_send.at[peer],
-            recv_sem=part_recv.at[peer], device_id={"grp": peer}, device_id_type=MESH,
-        )
-
-    def to_all(k):
-        peer = lax.rem(me_g + k, n_grp)
-        return pltpu.make_async_remote_copy(
-            src_ref=totals.at[me_g], dst_ref=totals.at[me_g], send_sem=total_send.at[peer],
-            recv_sem=total_recv.at[me_g], device_id={"grp": peer}, device_id_type=MESH,
-        )
-
-    def from_adder(k):
-        peer = lax.rem(me_g + k, n_grp)
-        return pltpu.make_async_remote_copy(
-            src_ref=totals.at[me_g], dst_ref=totals.at[peer], send_sem=total_send.at[peer],
-            recv_sem=total_recv.at[peer], device_id={"grp": peer}, device_id_type=MESH,
-        )
-
-    def loop(make, act):
-        def run(k, _):
-            getattr(make(k), act)()
-            return 0
-        lax.fori_loop(1, n_grp, run, 0)
-
-    loop(to_adder, "start")
-    gathered[me_g] = parts[me_g]
+    for k in (2, 1, 3):
+        in_team(k, True).start()
+    gathered[mine] = parts[mine]
+    for k in (2, 1, 3):
+        in_team(k, False).wait_recv()
+    totals[me_g] = (gathered[0] + gathered[1]) + (gathered[2] + gathered[3])
+    for k in (8, 7, 9, 6, 10, 5, 11, 4, 12, 3, 13, 2, 14, 1, 15):
+        to_all(k, True).start()
 
     high, low = halves(level)
     level_out[...] = mm(high, nodal_v[...], 1, 1) + mm(low, nodal_v[...], 1, 1)
-
-    loop(from_slab, "wait_recv")
-    totals[me_g] = jnp.sum(gathered[...], axis=0)
-    loop(to_all, "start")
     lax.fori_loop(1, n_dev, end_owner, 0)
-    loop(to_adder, "wait_send")
-    loop(from_adder, "wait_recv")
-
-    coarse = jnp.concatenate([totals[:, k, :] for k in range(3)], axis=1)
-    high, low = halves(coarse)
+    for k in (1, 2, 3):
+        in_team(k, True).wait_send()
+
+    def end_all(k, _):
+        to_all(k, False).wait_recv()
+        return 0
+
+    def end_sent(k, _):
+        to_all(k, True).wait_send()
+        return 0
+
+    lax.fori_loop(1, n_grp, end_all, 0)
+    coarse = []
+    for k in range(3):
+        quarters = []
+        for t in range(TEAM):
+            rows = [totals[TEAM * u + t, 4 * k:4 * k + 4, :] for u in range(n_grp // TEAM)]
+            quarters.append((rows[0] + rows[1]) + (rows[2] + rows[3]))
+        coarse.append(jnp.concatenate(quarters, axis=0))
+    high, low = halves(jnp.concatenate(coarse, axis=1))
     coarse_out[...] = mm(high, nodal_v[...], 1, 1) + mm(low, nodal_v[...], 1, 1)
-    loop(to_all, "wait_send")
+    lax.fori_loop(1, n_grp, end_sent, 0)
 
 
 def body(n_grp, n_dev, elem_stiff, density, owner, agg_slot, par_octant, agg_octant, coarse_map):
@@ -311,21 +313,21 @@
     dma = pltpu.SemaphoreType.DMA
     level, coarse = pl.pallas_call(
         functools.partial(kernel, n_grp, n_dev),
-        out_shape=(jax.ShapeDtypeStruct((64, 576), F32), jax.ShapeDtypeStruct((16, 576), F32)),
-        in_specs=[pl.BlockSpec(memory_space=pl.ANY)] * len(args),
+        out_shape=(pltpu.VMEM((64, 576), F32), pltpu.VMEM((16, 576), F32)),
+        in_specs=[pl.BlockSpec(memory_space=pltpu.HBM)] * len(args),
         out_specs=(pl.BlockSpec(memory_space=pltpu.VMEM), pl.BlockSpec(memory_space=pltpu.VMEM)),
         scratch_shapes=[pltpu.VMEM(a.shape, a.dtype) for a in args] + [
             pltpu.VMEM((8, 256, 512), BF16),
             pltpu.VMEM((n_dev, PACK, 128), F32),
             pltpu.VMEM((n_dev, PACK, 128), F32),
-            pltpu.VMEM((n_grp, 3, 128), F32),
-            pltpu.VMEM((n_grp, 3, 128), F32),
-            pltpu.VMEM((n_grp, 3, 128), F32),
-            dma((9,)), dma((8,)), dma((4,)), dma((n_dev,)), dma((n_dev,)),
-            dma((n_grp,)), dma((n_grp,)), dma((n_grp,)), dma((n_grp,)),
+            pltpu.VMEM((TEAM, 12, 128), F32),
+            pltpu.VMEM((TEAM, 12, 128), F32),
+            pltpu.VMEM((n_grp, 12, 128), F32),
+            dma((9,)), dma((1,)), dma((2,)), dma((n_dev,)), dma((n_dev,)),
+            dma((TEAM,)), dma((TEAM,)), dma((n_grp,)), dma((n_grp,)),
         ],
         compiler_params=pltpu.CompilerParams(
-            collective_id=0, has_side_effects=True, vmem_limit_bytes=48 * 1024 * 1024
+            collective_id=0, has_side_effects=True, vmem_limit_bytes=63 * 1024 * 1024
         ),
     )(*args)
     return level.T, coarse.T

time: 57.8 us -> 40.2 us (0.70)
  the two profiles are of different devices: /device:TPU:1 before, /device:TPU:6 now
where the time goes in v2:
time: 40.2 us; the launch traced here: 39.7 us
  Pallas kernels  37.8 us (94%)
  local copies, waits for them, and re-layouts  1.29 us (3%)
  between operations  0.64 us (2%)
    pallas_call x1, Pallas kernels, body(): pl.pallas_call(functools.partial(kernel, n_grp, n_dev), out_shape=(pltpu....  37.8 us
    unnamed x2, local copies, waits for them, and re-layouts  1.29 us

profile of v2, /device:TPU:6, one launch (start us, length us, event | category | flops | bytes accessed | tf_op | source)
XLA Modules:
  0.0 39.7 jit_solution(6022063628250176304)
XLA Ops:
  0.6 37.8 %shard_map.122 = (f32[64,576]{1,0:T(8,128)S(1)}, f32[16,576]{1,0:T(8,128)S(1)}) custom-call(bf16[576,2048]{1,0:T(8,128)(2,1)} %stiff.1, f32[1,2048]{1,0:T(1,128)} %bitcast.10, s32[1,256]{1,0:T(1,128)} %bitcast.11, s32[1,256]{1,0:T(1,128)} %bitcast.12, s32[1,256]{1,0:T(1,128)} %bitcast.13, s32[1,64]{1,0:T(1,128)} %bitcast.14, s32[1,64]{1,0:T(1,128)} %bitcast.15, ...), custom_call_target="tpu_custom_call" | custom-call | tf_op jit(solution)/shard_map/pallas_call | solution.py:314
  38.4 0.7 %copy.15 = f32[576,64]{0,1:T(8,128)} copy(f32[576,64]{0,1:T(8,128)S(1)} %bitcast.8) | data formatting | bytes 294912
  39.1 0.6 %copy.16 = f32[576,16]{0,1:T(8,128)} copy(f32[576,16]{0,1:T(8,128)S(1)} %bitcast.9) | data formatting | bytes 73728

commit v3 on v2

--- a/solution.py
+++ b/solution.py
@@ -21,7 +21,7 @@
     [(dx, dy, dc) for dx in range(4) for dy in range(4) for dc in range(2) if dx + dy + dc],
     key=lambda step: -(min(step[0], 4 - step[0]) + min(step[1], 4 - step[1])),
 )
-TEAM = 4
+HANDED = (8, 9, 10, 11, 12, 13, 14)
 PACK = 40
 
 
@@ -100,18 +100,21 @@
     me_g, me_d = lax.axis_index("grp"), lax.axis_index("dev")
     blocks = 8
 
-    loads = []
-    for index, (src, dst) in enumerate((
-        (dens, dens_v), (owner, owner_v), (slot, slot_v), (par_oct, par_oct_v), (agg_oct, agg_oct_v),
-        (agg_map, agg_map_v), (lift, lift_v), (signs, signs_v), (nodal, nodal_v),
-    )):
-        loads.append(pltpu.make_async_copy(src, dst, in_sem.at[index]))
+    small = [
+        pltpu.make_async_copy(src, dst, in_sem.at[index])
+        for index, (src, dst) in enumerate((
+            (dens, dens_v), (owner, owner_v), (slot, slot_v), (par_oct, par_oct_v),
+            (agg_oct, agg_oct_v), (agg_map, agg_map_v), (signs, signs_v),
+        ))
+    ]
+    lift_load = pltpu.make_async_copy(lift, lift_v, in_sem.at[7])
+    nodal_load = pltpu.make_async_copy(nodal, nodal_v, in_sem.at[8])
+    first_load = pltpu.make_async_copy(first, first_v, first_sem.at[0])
     stiff_loads = [
         pltpu.make_async_copy(stiff.at[:, pl.ds(1024 * c, 1024)], stiff_v.at[:, pl.ds(1024 * c, 1024)], stiff_sem.at[c])
         for c in range(2)
     ]
-    first_loads = [pltpu.make_async_copy(first, first_v, first_sem.at[0])]
-    for load in loads[:6] + stiff_loads + loads[6:8] + first_loads + loads[8:]:
+    for load in stiff_loads + small + [first_load, lift_load, nodal_load]:
         load.start()
 
     barrier = pltpu.get_barrier_semaphore()
@@ -121,14 +124,37 @@
         return 0
 
     def greet_grp(k, _):
-        pl.semaphore_signal(barrier, inc=1, device_id={"grp": lax.rem(me_g + k, n_grp)}, device_id_type=MESH)
+        pl.semaphore_signal(barrier, inc=1, device_id={"grp": k}, device_id_type=MESH)
         return 0
 
     lax.fori_loop(1, n_dev, greet_dev, 0)
-    lax.fori_loop(1, n_grp, greet_grp, 0)
-
-    for load in loads[:6]:
+
+    @pl.when(me_g == 0)
+    def _():
+        lax.fori_loop(1, n_grp, greet_grp, 0)
+
+    @pl.when((me_g >= 8) & (me_g <= 14))
+    def _():
+        greet_grp(15, 0)
+
+    @pl.when(((me_g >= 1) & (me_g <= 7)) | (me_g == 15))
+    def _():
+        greet_grp(0, 0)
+
+    pos = iota((256, 256), 0)
+    perm = ones_where(iota((256, 256), 1) == 8 * (pos % 32) + pos // 32)
+
+    def turn(b):
+        lanes = slice(256 * b, 256 * (b + 1))
+        block = jnp.concatenate([stiff_v[a:z, lanes] for a, z in KEEP], axis=0)
+        rows = mm(perm, block, 1, 1).astype(BF16)
+        for o in range(8):
+            xt[o, 32 * b:32 * (b + 1), :] = rows[32 * o:32 * (o + 1)]
+
+    for load in stiff_loads + small:
         load.wait()
+    for b in range(8):
+        turn(b)
 
     owner_row = owner_v[...]
     hits = iota((n_dev, 256), 0) == owner_row
@@ -138,8 +164,7 @@
     place = owner_row * SLOTS + rank.astype(jnp.int32)
     code = slot_v[...].astype(F32) + 1.0
 
-    pos = iota((256, 256), 0)
-    perm = ones_where(iota((256, 256), 1) == 8 * (pos % 32) + pos // 32)
+    picks = ones_where(iota((n_dev * SLOTS, 256), 0) == place)
 
     dens_row = dens_v[...]
     dens_8 = jnp.concatenate([dens_row[:, 256 * b:256 * (b + 1)] for b in range(blocks)], axis=0)
@@ -155,25 +180,16 @@
     own_row = iota((256, 256), 0) % 32 == iota((256, 256), 1) % 32
     weights = jnp.sum(jnp.where(own_row, spread_w, 0.0).reshape(8, 32, 256), axis=1)
 
-    for c in range(2):
-        stiff_loads[c].wait()
-        for b in range(4 * c, 4 * c + 4):
-            lanes = slice(256 * b, 256 * (b + 1))
-            block = jnp.concatenate([stiff_v[a:z, lanes] for a, z in KEEP], axis=0)
-            rows = mm(perm, block, 1, 1).astype(BF16)
-            for o in range(8):
-                xt[o, 32 * b:32 * (b + 1), :] = rows[32 * o:32 * (o + 1)]
-
+    octs = ones_where(iota((8, 256), 0) == par_oct_v[...])
+    flips = mm(signs_v[0:COLS, :], octs)
+
+    first_load.wait()
+    lift_load.wait()
     parent = None
-    first_loads[0].wait()
-    for load in loads[6:8]:
-        load.wait()
     for o in range(8):
         term = mm(first_v[o], xt[o], 1, 1) * weights[o:o + 1, :]
         parent = term if parent is None else parent + term
 
-    octs = ones_where(iota((8, 256), 0) == par_oct_v[...])
-    flips = mm(signs_v[0:COLS, :], octs)
     high, low = halves(parent * flips)
     lift_c = lift_v[0:COLS, 0:COLS]
     sent = (mm(lift_c, high) + mm(lift_c, low)) * flips
@@ -183,14 +199,19 @@
     full = jnp.concatenate([sent, gap, tail, gap], axis=0)
     high, low = halves(full)
 
-    picks = ones_where(iota((n_dev * SLOTS, 256), 0) == place)
     chosen = mm(picks, high, 1, 1) + mm(picks, low, 1, 1)
     outgo[:, 0:16, :] = chosen[:, 0:128].reshape(n_dev, 16, 128)
     outgo[:, 16:32, :] = chosen[:, 128:256].reshape(n_dev, 16, 128)
     ends = chosen[:, 256:384].reshape(n_dev, 2, 8, 128)
     outgo[:, 32:40, :] = jnp.where(iota((n_dev, 8, 128), 2) < 64, ends[:, 0], ends[:, 1])
 
-    pl.semaphore_wait(barrier, n_dev + n_grp - 2)
+    @pl.when((me_g == 0) | (me_g == 15))
+    def _():
+        pl.semaphore_wait(barrier, n_dev - 1 + 8)
+
+    @pl.when((me_g >= 1) & (me_g <= 14))
+    def _():
+        pl.semaphore_wait(barrier, n_dev)
 
     def to_owner(peer):
         return pltpu.make_async_remote_copy(
@@ -220,7 +241,7 @@
     octs = ones_where(iota((8, 64), 0) == agg_oct_v[...])
     agg_flips = mm(octs, signs_v[...], 0, 1)
     sums = ones_where(iota((16, 64), 0) == agg_map_v[...])
-    loads[8].wait()
+    nodal_load.wait()
 
     lax.fori_loop(1, n_dev, end_source, 0)
 
@@ -246,61 +267,71 @@
     lifted = mm(both, lift_v[...], 1, 1)
     high, low = halves((lifted[0:64] + lifted[64:128]) * agg_flips)
     share = mm(sums, high) + mm(sums, low)
-    for t in range(TEAM):
-        for k in range(3):
-            parts[t, 4 * k:4 * k + 4, :] = share[4 * t:4 * t + 4, 128 * k:128 * (k + 1)]
-
-    mine = lax.rem(me_g, TEAM)
-    base = me_g - mine
-
-    def in_team(k, sending):
-        other = lax.rem(mine + k, TEAM)
+    parts[0:16, :] = share[:, 0:128]
+    parts[16:32, :] = share[:, 128:256]
+    parts[32:40, :] = jnp.where(iota((8, 128), 1) < 64, share[0:8, 256:384], pltpu.roll(share[8:16, 256:384], 64, 1))
+
+    def to_root(source):
         return pltpu.make_async_remote_copy(
-            src_ref=parts.at[other], dst_ref=gathered.at[mine if sending else other], send_sem=part_send.at[other],
-            recv_sem=part_recv.at[mine if sending else other], device_id={"grp": base + other}, device_id_type=MESH,
+            src_ref=parts, dst_ref=gathered.at[source], send_sem=part_send.at[0],
+            recv_sem=part_recv.at[source], device_id={"grp": 0}, device_id_type=MESH,
         )
 
-    def to_all(k, sending):
-        peer = lax.rem(me_g + k, n_grp)
+    def from_root(target):
         return pltpu.make_async_remote_copy(
-            src_ref=totals.at[me_g], dst_ref=totals.at[me_g if sending else peer], send_sem=total_send.at[peer],
-            recv_sem=total_recv.at[me_g if sending else peer], device_id={"grp": peer}, device_id_type=MESH,
+            src_ref=totals, dst_ref=totals, send_sem=total_send.at[target],
+            recv_sem=total_recv.at[0], device_id={"grp": target}, device_id_type=MESH,
         )
 
-    for k in (2, 1, 3):
-        in_team(k, True).start()
-    gathered[mine] = parts[mine]
-    for k in (2, 1, 3):
-        in_team(k, False).wait_recv()
-    totals[me_g] = (gathered[0] + gathered[1]) + (gathered[2] + gathered[3])
-    for k in (8, 7, 9, 6, 10, 5, 11, 4, 12, 3, 13, 2, 14, 1, 15):
-        to_all(k, True).start()
+    @pl.when(me_g > 0)
+    def _():
+        to_root(me_g).start()
 
     high, low = halves(level)
     level_out[...] = mm(high, nodal_v[...], 1, 1) + mm(low, nodal_v[...], 1, 1)
     lax.fori_loop(1, n_dev, end_owner, 0)
-    for k in (1, 2, 3):
-        in_team(k, True).wait_send()
-
-    def end_all(k, _):
-        to_all(k, False).wait_recv()
-        return 0
-
-    def end_sent(k, _):
-        to_all(k, True).wait_send()
-        return 0
-
-    lax.fori_loop(1, n_grp, end_all, 0)
-    coarse = []
-    for k in range(3):
-        quarters = []
-        for t in range(TEAM):
-            rows = [totals[TEAM * u + t, 4 * k:4 * k + 4, :] for u in range(n_grp // TEAM)]
-            quarters.append((rows[0] + rows[1]) + (rows[2] + rows[3]))
-        coarse.append(jnp.concatenate(quarters, axis=0))
-    high, low = halves(jnp.concatenate(coarse, axis=1))
+
+    @pl.when(me_g == 0)
+    def _():
+        def end_part(k, _):
+            to_root(k).wait_recv()
+            return 0
+
+        lax.fori_loop(1, n_grp, end_part, 0)
+        sums = [parts[...]] + [gathered[k] for k in range(1, n_grp)]
+        while len(sums) > 1:
+            sums = [sums[k] + sums[k + 1] for k in range(0, len(sums), 2)]
+        totals[...] = sums[0]
+        for k in (1, 2, 15, 3, 4, 5, 6, 7):
+            from_root(k).start()
+
+    @pl.when(me_g > 0)
+    def _():
+        from_root(me_g).wait_recv()
+
+    @pl.when(me_g == 15)
+    def _():
+        for k in HANDED:
+            from_root(k).start()
+
+    ends = totals[32:40, :]
+    ends = jnp.concatenate([ends, pltpu.roll(ends, 64, 1)], axis=0)
+    high, low = halves(jnp.concatenate([totals[0:16, :], totals[16:32, :], ends], axis=1))
     coarse_out[...] = mm(high, nodal_v[...], 1, 1) + mm(low, nodal_v[...], 1, 1)
-    lax.fori_loop(1, n_grp, end_sent, 0)
+
+    @pl.when(me_g > 0)
+    def _():
+        to_root(me_g).wait_send()
+
+    @pl.when(me_g == 0)
+    def _():
+        for k in (1, 2, 15, 3, 4, 5, 6, 7):
+            from_root(k).wait_send()
+
+    @pl.when(me_g == 15)
+    def _():
+        for k in HANDED:
+            from_root(k).wait_send()
 
 
 def body(n_grp, n_dev, elem_stiff, density, owner, agg_slot, par_octant, agg_octant, coarse_map):
@@ -320,11 +351,11 @@
             pltpu.VMEM((8, 256, 512), BF16),
             pltpu.VMEM((n_dev, PACK, 128), F32),
             pltpu.VMEM((n_dev, PACK, 128), F32),
-            pltpu.VMEM((TEAM, 12, 128), F32),
-            pltpu.VMEM((TEAM, 12, 128), F32),
-            pltpu.VMEM((n_grp, 12, 128), F32),
+            pltpu.VMEM((PACK, 128), F32),
+            pltpu.VMEM((n_grp, PACK, 128), F32),
+            pltpu.VMEM((PACK, 128), F32),
             dma((9,)), dma((1,)), dma((2,)), dma((n_dev,)), dma((n_dev,)),
-            dma((TEAM,)), dma((TEAM,)), dma((n_grp,)), dma((n_grp,)),
+            dma((1,)), dma((n_grp,)), dma((n_grp,)), dma((1,)),
         ],
         compiler_params=pltpu.CompilerParams(
             collective_id=0, has_side_effects=True, vmem_limit_bytes=63 * 1024 * 1024

time: 40.2 us -> 38.8 us (0.965)
  Pallas kernels: 37.8 us -> 36.7 us
    pallas_call x1, Pallas kernels: 37.8 us -> 36.7 us  [body(): pl.pallas_call(functools.partial(kernel, n_grp, n_dev), out_shape=(pltpu....]
where the time goes in v3:
time: 38.8 us; the launch traced here: 38.6 us
  Pallas kernels  36.7 us (95%)
  local copies, waits for them, and re-layouts  1.29 us (3%)
  between operations  0.64 us (2%)
    pallas_call x1, Pallas kernels, body(): pl.pallas_call(functools.partial(kernel, n_grp, n_dev), out_shape=(pltpu....  36.7 us
    unnamed x2, local copies, waits for them, and re-layouts  1.29 us

profile of v3, /device:TPU:6, one launch (start us, length us, event | category | flops | bytes accessed | tf_op | source)
XLA Modules:
  0.0 38.6 jit_solution(6646951850315419804)
XLA Ops:
  0.6 36.7 %shard_map.122 = (f32[64,576]{1,0:T(8,128)S(1)}, f32[16,576]{1,0:T(8,128)S(1)}) custom-call(bf16[576,2048]{1,0:T(8,128)(2,1)} %stiff.1, f32[1,2048]{1,0:T(1,128)} %bitcast.10, s32[1,256]{1,0:T(1,128)} %bitcast.11, s32[1,256]{1,0:T(1,128)} %bitcast.12, s32[1,256]{1,0:T(1,128)} %bitcast.13, s32[1,64]{1,0:T(1,128)} %bitcast.14, s32[1,64]{1,0:T(1,128)} %bitcast.15, ...), custom_call_target="tpu_custom_call" | custom-call | tf_op jit(solution)/shard_map/pallas_call | solution.py:345
  37.4 0.7 %copy.15 = f32[576,64]{0,1:T(8,128)} copy(f32[576,64]{0,1:T(8,128)S(1)} %bitcast.8) | data formatting | bytes 294912
  38.0 0.6 %copy.16 = f32[576,16]{0,1:T(8,128)} copy(f32[576,16]{0,1:T(8,128)S(1)} %bitcast.9) | data formatting | bytes 73728

commit v4 on v3

--- a/solution.py
+++ b/solution.py
@@ -215,23 +215,14 @@
 
     def to_owner(peer):
         return pltpu.make_async_remote_copy(
-            src_ref=outgo.at[peer], dst_ref=income.at[me_d], send_sem=send_sem.at[peer],
-            recv_sem=recv_sem.at[me_d], device_id={"dev": peer}, device_id_type=MESH,
+            src_ref=outgo.at[peer], dst_ref=income.at[me_d], send_sem=send_sem.at[0],
+            recv_sem=recv_sem.at[0], device_id={"dev": peer}, device_id_type=MESH,
         )
 
-    def from_source(peer):
-        return pltpu.make_async_remote_copy(
-            src_ref=outgo.at[peer], dst_ref=income.at[peer], send_sem=send_sem.at[peer],
-            recv_sem=recv_sem.at[peer], device_id={"dev": peer}, device_id_type=MESH,
-        )
-
-    def end_source(k, _):
-        from_source(lax.rem(me_d + k, n_dev)).wait_recv()
-        return 0
-
-    def end_owner(k, _):
-        to_owner(lax.rem(me_d + k, n_dev)).wait_send()
-        return 0
+    every_owner = pltpu.make_async_remote_copy(
+        src_ref=outgo.at[pl.ds(0, n_dev - 1)], dst_ref=income.at[pl.ds(0, n_dev - 1)], send_sem=send_sem.at[0],
+        recv_sem=recv_sem.at[0], device_id={"dev": lax.rem(me_d + 1, n_dev)}, device_id_type=MESH,
+    )
 
     x, y, core = lax.div(me_d, 8), lax.rem(lax.div(me_d, 2), 4), lax.rem(me_d, 2)
     for dx, dy, dc in FAR_FIRST:
@@ -243,7 +234,7 @@
     sums = ones_where(iota((16, 64), 0) == agg_map_v[...])
     nodal_load.wait()
 
-    lax.fori_loop(1, n_dev, end_source, 0)
+    every_owner.wait_recv()
 
     lane = iota((8, 128), 1)
     code_at = ones_where(lane == CODE - 256 + 64 * iota((8, 128), 0))
@@ -274,7 +265,7 @@
     def to_root(source):
         return pltpu.make_async_remote_copy(
             src_ref=parts, dst_ref=gathered.at[source], send_sem=part_send.at[0],
-            recv_sem=part_recv.at[source], device_id={"grp": 0}, device_id_type=MESH,
+            recv_sem=part_recv.at[0], device_id={"grp": 0}, device_id_type=MESH,
         )
 
     def from_root(target):
@@ -289,15 +280,14 @@
 
     high, low = halves(level)
     level_out[...] = mm(high, nodal_v[...], 1, 1) + mm(low, nodal_v[...], 1, 1)
-    lax.fori_loop(1, n_dev, end_owner, 0)
+    every_owner.wait_send()
 
     @pl.when(me_g == 0)
     def _():
-        def end_part(k, _):
-            to_root(k).wait_recv()
-            return 0
-
-        lax.fori_loop(1, n_grp, end_part, 0)
+        pltpu.make_async_remote_copy(
+            src_ref=gathered.at[pl.ds(1, n_grp - 1)], dst_ref=gathered.at[pl.ds(1, n_grp - 1)], send_sem=part_send.at[0],
+            recv_sem=part_recv.at[0], device_id={"grp": 1}, device_id_type=MESH,
+        ).wait_recv()
         sums = [parts[...]] + [gathered[k] for k in range(1, n_grp)]
         while len(sums) > 1:
             sums = [sums[k] + sums[k + 1] for k in range(0, len(sums), 2)]
@@ -354,8 +344,8 @@
             pltpu.VMEM((PACK, 128), F32),
             pltpu.VMEM((n_grp, PACK, 128), F32),
             pltpu.VMEM((PACK, 128), F32),
-            dma((9,)), dma((1,)), dma((2,)), dma((n_dev,)), dma((n_dev,)),
-            dma((1,)), dma((n_grp,)), dma((n_grp,)), dma((1,)),
+            dma((9,)), dma((1,)), dma((2,)), dma((1,)), dma((1,)),
+            dma((1,)), dma((1,)), dma((n_grp,)), dma((1,)),
         ],
         compiler_params=pltpu.CompilerParams(
             collective_id=0, has_side_effects=True, vmem_limit_bytes=63 * 1024 * 1024

time: 38.8 us -> 37.8 us (0.974)
  Pallas kernels: 36.7 us -> 35.8 us
    pallas_call x1, Pallas kernels: 36.7 us -> 35.8 us  [body(): pl.pallas_call(functools.partial(kernel, n_grp, n_dev), out_shape=(pltpu....]
where the time goes in v4:
time: 37.8 us; the launch traced here: 37.7 us
  Pallas kernels  35.8 us (95%)
  local copies, waits for them, and re-layouts  1.29 us (3%)
  between operations  0.64 us (2%)
    pallas_call x1, Pallas kernels, body(): pl.pallas_call(functools.partial(kernel, n_grp, n_dev), out_shape=(pltpu....  35.8 us
    unnamed x2, local copies, waits for them, and re-layouts  1.29 us

profile of v4, /device:TPU:6, one launch (start us, length us, event | category | flops | bytes accessed | tf_op | source)
XLA Modules:
  0.0 37.7 jit_solution(10374236798459960343)
XLA Ops:
  0.6 35.8 %shard_map.122 = (f32[64,576]{1,0:T(8,128)S(1)}, f32[16,576]{1,0:T(8,128)S(1)}) custom-call(bf16[576,2048]{1,0:T(8,128)(2,1)} %stiff.1, f32[1,2048]{1,0:T(1,128)} %bitcast.10, s32[1,256]{1,0:T(1,128)} %bitcast.11, s32[1,256]{1,0:T(1,128)} %bitcast.12, s32[1,256]{1,0:T(1,128)} %bitcast.13, s32[1,64]{1,0:T(1,128)} %bitcast.14, s32[1,64]{1,0:T(1,128)} %bitcast.15, ...), custom_call_target="tpu_custom_call" | custom-call | tf_op jit(solution)/shard_map/pallas_call | solution.py:335
  36.4 0.7 %copy.15 = f32[576,64]{0,1:T(8,128)} copy(f32[576,64]{0,1:T(8,128)S(1)} %bitcast.8) | data formatting | bytes 294912
  37.1 0.6 %copy.16 = f32[576,16]{0,1:T(8,128)} copy(f32[576,16]{0,1:T(8,128)S(1)} %bitcast.9) | data formatting | bytes 73728

commit v5 on v4

--- a/solution.py
+++ b/solution.py
@@ -199,7 +199,7 @@
     full = jnp.concatenate([sent, gap, tail, gap], axis=0)
     high, low = halves(full)
 
-    chosen = mm(picks, high, 1, 1) + mm(picks, low, 1, 1)
+    chosen = mm(jnp.concatenate([picks, picks], axis=1), jnp.concatenate([high, low], axis=1), 1, 1)
     outgo[:, 0:16, :] = chosen[:, 0:128].reshape(n_dev, 16, 128)
     outgo[:, 16:32, :] = chosen[:, 128:256].reshape(n_dev, 16, 128)
     ends = chosen[:, 256:384].reshape(n_dev, 2, 8, 128)
@@ -249,7 +249,7 @@
             packed,
         ], axis=1)
         high, low = halves(wide)
-        level.append(mm(into, high) + mm(into, low))
+        level.append(mm(jnp.concatenate([into, into], axis=1), jnp.concatenate([high, low], axis=0)))
     ends = level[0][:, 256:] + pltpu.roll(level[1][:, 256:], 64, 1)
     ends = jnp.where(iota((64, 128), 1) < MODES - 256, ends, 0.0)
     level = jnp.concatenate([level[0][:, :256] + level[1][:, :256], ends], axis=1)
@@ -257,7 +257,7 @@
     both = jnp.concatenate(halves(level * agg_flips), axis=0)
     lifted = mm(both, lift_v[...], 1, 1)
     high, low = halves((lifted[0:64] + lifted[64:128]) * agg_flips)
-    share = mm(sums, high) + mm(sums, low)
+    share = mm(jnp.concatenate([sums, sums], axis=1), jnp.concatenate([high, low], axis=0))
     parts[0:16, :] = share[:, 0:128]
     parts[16:32, :] = share[:, 128:256]
     parts[32:40, :] = jnp.where(iota((8, 128), 1) < 64, share[0:8, 256:384], pltpu.roll(share[8:16, 256:384], 64, 1))
@@ -279,7 +279,8 @@
         to_root(me_g).start()
 
     high, low = halves(level)
-    level_out[...] = mm(high, nodal_v[...], 1, 1) + mm(low, nodal_v[...], 1, 1)
+    both = mm(jnp.concatenate([high, low], axis=0), nodal_v[...], 1, 1)
+    level_out[...] = both[0:64] + both[64:128]
     every_owner.wait_send()
 
     @pl.when(me_g == 0)
@@ -307,7 +308,8 @@
     ends = totals[32:40, :]
     ends = jnp.concatenate([ends, pltpu.roll(ends, 64, 1)], axis=0)
     high, low = halves(jnp.concatenate([totals[0:16, :], totals[16:32, :], ends], axis=1))
-    coarse_out[...] = mm(high, nodal_v[...], 1, 1) + mm(low, nodal_v[...], 1, 1)
+    both = mm(jnp.concatenate([high, low], axis=0), nodal_v[...], 1, 1)
+    coarse_out[...] = both[0:16] + both[16:32]
 
     @pl.when(me_g > 0)
     def _():

time: 37.8 us -> 37.6 us (level)
  no operation moved by 1% of the time
where the time goes in v5:
time: 37.6 us; the launch traced here: 37.4 us
  Pallas kernels  35.5 us (94%)
  local copies, waits for them, and re-layouts  1.29 us (3%)
  between operations  0.64 us (2%)
    pallas_call x1, Pallas kernels, body(): pl.pallas_call(functools.partial(kernel, n_grp, n_dev), out_shape=(pltpu....  35.5 us
    unnamed x2, local copies, waits for them, and re-layouts  1.29 us

profile of v5, /device:TPU:6, one launch (start us, length us, event | category | flops | bytes accessed | tf_op | source)
XLA Modules:
  0.0 37.4 jit_solution(2209480619579773017)
XLA Ops:
  0.6 35.5 %shard_map.122 = (f32[64,576]{1,0:T(8,128)S(1)}, f32[16,576]{1,0:T(8,128)S(1)}) custom-call(bf16[576,2048]{1,0:T(8,128)(2,1)} %stiff.1, f32[1,2048]{1,0:T(1,128)} %bitcast.10, s32[1,256]{1,0:T(1,128)} %bitcast.11, s32[1,256]{1,0:T(1,128)} %bitcast.12, s32[1,256]{1,0:T(1,128)} %bitcast.13, s32[1,64]{1,0:T(1,128)} %bitcast.14, s32[1,64]{1,0:T(1,128)} %bitcast.15, ...), custom_call_target="tpu_custom_call" | custom-call | tf_op jit(solution)/shard_map/pallas_call | solution.py:337
  36.2 0.7 %copy.15 = f32[576,64]{0,1:T(8,128)} copy(f32[576,64]{0,1:T(8,128)S(1)} %bitcast.8) | data formatting | bytes 294912
  36.8 0.6 %copy.16 = f32[576,16]{0,1:T(8,128)} copy(f32[576,16]{0,1:T(8,128)S(1)} %bitcast.9) | data formatting | bytes 73728

commit v6 on v5

--- a/solution.py
+++ b/solution.py
@@ -54,7 +54,7 @@
         modes = table[octant] @ basis
         term = modes[row_i][:, ks].T * modes[row_j][:, ls].T
         swap = modes[row_j][:, ks].T * modes[row_i][:, ls].T
-        first[octant, :MODES] = np.where(used[None, :], term + off * swap, 0.0)
+        first[octant, :MODES] = np.where(used[None, :], term + off * swap, 0.0) / 64.0
     step = np.linalg.inv(basis) @ table[7] @ basis
     lift = np.zeros((WIDE, WIDE))
     lift[:MODES, :MODES] = step[ks][:, ks].T * step[ls][:, ls].T + (ks != ls)[None, :] * (step[ls][:, ks].T * step[ks][:, ls].T)
@@ -67,7 +67,7 @@
         signs[:MODES, octant] = sign
     nodal = np.zeros((576, WIDE))
     a, b = np.arange(576) // 24, np.arange(576) % 24
-    nodal[:, :MODES] = (basis[a][:, ks] * basis[b][:, ls] + (ks != ls)[None, :] * basis[a][:, ls] * basis[b][:, ks]) / 64.0
+    nodal[:, :MODES] = basis[a][:, ks] * basis[b][:, ls] + (ks != ls)[None, :] * basis[a][:, ls] * basis[b][:, ks]
     cast = lambda array: np.asarray(array).astype(ml_dtypes.bfloat16)
     return cast(first), cast(lift), cast(signs), cast(nodal)
 

time: 37.6 us -> 37.6 us (level)
  no operation moved by 1% of the time
where the time goes in v6:
time: 37.6 us; the launch traced here: 37.4 us
  Pallas kernels  35.5 us (94%)
  local copies, waits for them, and re-layouts  1.29 us (3%)
  between operations  0.64 us (2%)
    pallas_call x1, Pallas kernels, body(): pl.pallas_call(functools.partial(kernel, n_grp, n_dev), out_shape=(pltpu....  35.5 us
    unnamed x2, local copies, waits for them, and re-layouts  1.29 us

profile of v6, /device:TPU:6, one launch (start us, length us, event | category | flops | bytes accessed | tf_op | source)
XLA Modules:
  0.0 37.4 jit_solution(6517046377380455056)
XLA Ops:
  0.6 35.5 %shard_map.122 = (f32[64,576]{1,0:T(8,128)S(1)}, f32[16,576]{1,0:T(8,128)S(1)}) custom-call(bf16[576,2048]{1,0:T(8,128)(2,1)} %stiff.1, f32[1,2048]{1,0:T(1,128)} %bitcast.10, s32[1,256]{1,0:T(1,128)} %bitcast.11, s32[1,256]{1,0:T(1,128)} %bitcast.12, s32[1,256]{1,0:T(1,128)} %bitcast.13, s32[1,64]{1,0:T(1,128)} %bitcast.14, s32[1,64]{1,0:T(1,128)} %bitcast.15, ...), custom_call_target="tpu_custom_call" | custom-call | tf_op jit(solution)/shard_map/pallas_call | solution.py:337
  36.2 0.7 %copy.15 = f32[576,64]{0,1:T(8,128)} copy(f32[576,64]{0,1:T(8,128)S(1)} %bitcast.8) | data formatting | bytes 294912
  36.8 0.6 %copy.16 = f32[576,16]{0,1:T(8,128)} copy(f32[576,16]{0,1:T(8,128)S(1)} %bitcast.9) | data formatting | bytes 73728

commit v7 on v6

--- a/solution.py
+++ b/solution.py
@@ -110,11 +110,8 @@
     lift_load = pltpu.make_async_copy(lift, lift_v, in_sem.at[7])
     nodal_load = pltpu.make_async_copy(nodal, nodal_v, in_sem.at[8])
     first_load = pltpu.make_async_copy(first, first_v, first_sem.at[0])
-    stiff_loads = [
-        pltpu.make_async_copy(stiff.at[:, pl.ds(1024 * c, 1024)], stiff_v.at[:, pl.ds(1024 * c, 1024)], stiff_sem.at[c])
-        for c in range(2)
-    ]
-    for load in stiff_loads + small + [first_load, lift_load, nodal_load]:
+    stiff_load = pltpu.make_async_copy(stiff, stiff_v, stiff_sem.at[0])
+    for load in [stiff_load] + small + [first_load, lift_load, nodal_load]:
         load.start()
 
     barrier = pltpu.get_barrier_semaphore()
@@ -151,7 +148,7 @@
         for o in range(8):
             xt[o, 32 * b:32 * (b + 1), :] = rows[32 * o:32 * (o + 1)]
 
-    for load in stiff_loads + small:
+    for load in [stiff_load] + small[:4] + small[6:]:
         load.wait()
     for b in range(8):
         turn(b)
@@ -191,8 +188,9 @@
         parent = term if parent is None else parent + term
 
     high, low = halves(parent * flips)
-    lift_c = lift_v[0:COLS, 0:COLS]
-    sent = (mm(lift_c, high) + mm(lift_c, low)) * flips
+    lift_c = lift_v[0:COLS, :]
+    gap = jnp.zeros((WIDE - COLS, 256), BF16)
+    sent = mm(jnp.concatenate([lift_c, lift_c], axis=1), jnp.concatenate([high, gap, low, gap], axis=0)) * flips
     sent = jnp.where(iota((COLS, 256), 0) == CODE, code, sent)
     tail = sent[256:COLS]
     gap = jnp.zeros((16, 256), F32)
@@ -229,6 +227,8 @@
         to_owner((lax.rem(x + dx, 4) * 4 + lax.rem(y + dy, 4)) * 2 + lax.rem(core + dc, 2)).start()
     income[me_d] = outgo[me_d]
 
+    for load in small[4:6]:
+        load.wait()
     octs = ones_where(iota((8, 64), 0) == agg_oct_v[...])
     agg_flips = mm(octs, signs_v[...], 0, 1)
     sums = ones_where(iota((16, 64), 0) == agg_map_v[...])
@@ -346,7 +346,7 @@
             pltpu.VMEM((PACK, 128), F32),
             pltpu.VMEM((n_grp, PACK, 128), F32),
             pltpu.VMEM((PACK, 128), F32),
-            dma((9,)), dma((1,)), dma((2,)), dma((1,)), dma((1,)),
+            dma((9,)), dma((1,)), dma((1,)), dma((1,)), dma((1,)),
             dma((1,)), dma((1,)), dma((n_grp,)), dma((1,)),
         ],
         compiler_params=pltpu.CompilerParams(

time: 37.6 us -> 37.5 us (level)
  no operation moved by 1% of the time
where the time goes in v7:
time: 37.5 us; the launch traced here: 37.4 us
  Pallas kernels  35.4 us (94%)
  local copies, waits for them, and re-layouts  1.29 us (3%)
  between operations  0.64 us (2%)
    pallas_call x1, Pallas kernels, body(): pl.pallas_call(functools.partial(kernel, n_grp, n_dev), out_shape=(pltpu....  35.4 us
    unnamed x2, local copies, waits for them, and re-layouts  1.29 us

profile of v7, /device:TPU:6, one launch (start us, length us, event | category | flops | bytes accessed | tf_op | source)
XLA Modules:
  0.0 37.4 jit_solution(5263719233190112299)
XLA Ops:
  0.6 35.4 %shard_map.122 = (f32[64,576]{1,0:T(8,128)S(1)}, f32[16,576]{1,0:T(8,128)S(1)}) custom-call(bf16[576,2048]{1,0:T(8,128)(2,1)} %stiff.1, f32[1,2048]{1,0:T(1,128)} %bitcast.10, s32[1,256]{1,0:T(1,128)} %bitcast.11, s32[1,256]{1,0:T(1,128)} %bitcast.12, s32[1,256]{1,0:T(1,128)} %bitcast.13, s32[1,64]{1,0:T(1,128)} %bitcast.14, s32[1,64]{1,0:T(1,128)} %bitcast.15, ...), custom_call_target="tpu_custom_call" | custom-call | tf_op jit(solution)/shard_map/pallas_call | solution.py:337
  36.1 0.7 %copy.15 = f32[576,64]{0,1:T(8,128)} copy(f32[576,64]{0,1:T(8,128)S(1)} %bitcast.8) | data formatting | bytes 294912
  36.7 0.6 %copy.16 = f32[576,16]{0,1:T(8,128)} copy(f32[576,16]{0,1:T(8,128)S(1)} %bitcast.9) | data formatting | bytes 73728
